TPU v7x, 32 devices: a whole 2x2x4 slice. The times are simulated.
32 devices in a mesh: scen: 4 (over y, x), row: 4 (over z), col: 2 (over core).
Axes of the slice: x: 2, y: 2, z: 4, core: 2. Of those that a mesh axis runs over, the one named last changes fastest.
Arguments:
- border: bfloat16 [16, 4, 512, 512], P('scen', None, ('row', 'col')), may hold values from -4.5 to 4.5, as said below
- panel_border: bfloat16 [16, 512, 512], P('scen'), may hold values from -0.26516504 to 0.26516504
- kinv: bfloat16 [16, 512, 512], P('scen'), may hold values from -1 to 4, as said below
- factor: bfloat16 [2048, 4096], P(('scen', 'row'), 'col'), may hold values from -4.5 to 4.5
- root_block: float32 [2048, 512], P(('scen', 'row', 'col')), may hold values from -9 to 43, as said below
Outputs:
- panel_factor: float32 [2048, 512], P(('scen', 'row', 'col'))
Inputs may be any that keep to these rules, and one draw needn't show every extreme that they name: border[s, 0] is panel_border[s] transposed. `kinv`: each scenario's matrix is symmetric positive definite up to rounding, with eigenvalues 0.5 or more. `root_block`: its first 512 rows form a symmetric matrix; schur[0:512] is positive definite.
All inputs are finite; a program needn't handle non-finite values.
Results may differ from a plain program's by a relative error of at most 0.0025.
Values may be sent and summed in bfloat16 or wider, within the bound.
A program may use at most 128 MiB of HBM per device.

v0:
```python
import functools

import jax
import jax.numpy as jnp
from jax import lax
from jax.experimental import pallas as pl
from jax.experimental.pallas import tpu as pltpu
from jax.sharding import PartitionSpec as P

MESH = pl.DeviceIdType.MESH
F32 = jnp.float32
BLOCK = 128
STRIP = 16
SLICES = 4


def mm(a, b, da, db):
    return lax.dot_general(a, b, (((da,), (db,)), ((), ())), preferred_element_type=F32)


def split(x):
    high = x.astype(jnp.bfloat16)
    left = x - high.astype(F32)
    middle = left.astype(jnp.bfloat16)
    return high, middle, (left - middle.astype(F32)).astype(jnp.bfloat16)


def mm_f32(a, b, da, db):
    ah, am, al = split(a)
    bh, bm, bl = split(b)
    return mm(
        jnp.concatenate([al, am, ah, am, ah, ah], axis=da),
        jnp.concatenate([bh, bm, bl, bh, bm, bh], axis=db),
        da, db,
    )


def panel_kernel(
    S, R, C, slices,
    border_hbm, pb_hbm, kinv_hbm, factor_hbm, root_hbm, out_ref,
    border, pb, kinv, factor, root,
    lead, roots, solved, part, part_in, cp, rs_a, dp, rs_b, columns, upd, upd_in, rest, aug, work, inv,
    in_sem, f_send, f_recv, line_send, line_recv, p_send, p_recv,
    a_send, a_recv, b_send, b_recv, g_send, g_recv,
    u_send, u_recv,
):
    s, r, c = lax.axis_index("scen"), lax.axis_index("row"), lax.axis_index("col")
    rows, depth = factor.shape
    own, panel = root.shape
    wide = depth // slices
    blocks = panel // BLOCK
    scenarios = kinv.shape[0]
    share = scenarios // C
    groups = cp.shape[0]
    half = BLOCK // C
    n = rs_b.shape[2]
    owners = half // n
    parts = 2
    piece = rows // parts

    def peer_s(o):
        return lax.rem(s + o, S)

    def fetch(k):
        src, dst = (
            (factor_hbm, factor), (root_hbm, root), (pb_hbm, pb), (kinv_hbm, kinv), (border_hbm, border)
        )[k]
        return pltpu.make_async_copy(src, dst, in_sem.at[k])

    for k in range(5):
        fetch(k).start()

    barrier = pltpu.get_barrier_semaphore()
    for o in range(1, S):
        pl.semaphore_signal(barrier, inc=1, device_id=(peer_s(o), r, c), device_id_type=MESH)
        pl.semaphore_signal(barrier, inc=1, device_id=(peer_s(o), r, 1 - c), device_id_type=MESH)
    for o in range(1, R):
        pl.semaphore_signal(barrier, inc=1, device_id=(s, lax.rem(r + o, R), c), device_id_type=MESH)
    pl.semaphore_signal(barrier, inc=1, device_id=(s, r, 1 - c), device_id_type=MESH)
    pl.semaphore_wait(barrier, C * (S - 1) + R)

    def remote(src, dst, send, recv, to):
        return pltpu.make_async_remote_copy(
            src_ref=src, dst_ref=dst, send_sem=send, recv_sem=recv, device_id=to, device_id_type=MESH
        )

    def mine_of(q):
        return pl.ds(pl.multiple_of(q * rows, rows), rows)

    def f_copy(j):
        return remote(
            factor_hbm.at[:, j * wide:(j + 1) * wide], columns.at[s], f_send.at[j], f_recv.at[s],
            (j, r, c),
        )

    def f_start():
        for j in range(slices):
            @pl.when(s != j)
            def _():
                f_copy(j).start()

    def f_arrived(q):
        remote(columns.at[q], columns.at[q], f_send.at[0], f_recv.at[q], (s, r, 1 - c)).wait_recv()

    def line_copy(kind, q, up):
        if kind == parts:
            ref = roots.at[q]
        else:
            ref = lead.at[pl.ds(pl.multiple_of(q * rows + kind * piece, piece), piece), :]
        return remote(
            ref, ref, line_send.at[kind, q, 1 if up else 0], line_recv.at[kind, q],
            (s, lax.rem(r + (1 if up else R - 1), R), c),
        )

    def line_start(kind, q, up):
        @pl.when(r < R - 1 if up else r > 0)
        def _():
            line_copy(kind, q, up).start()

    def hop(kind, d):
        @pl.when(s < (1 if kind == parts else slices))
        def _():
            @pl.when(r >= d)
            def _():
                line_copy(kind, r - d, True).wait_recv()
                line_start(kind, r - d, True)

            @pl.when(r + d < R)
            def _():
                line_copy(kind, r + d, False).wait_recv()
                line_start(kind, r + d, False)

    def line_sent(kind):
        @pl.when(s < (1 if kind == parts else slices))
        def _():
            for d in range(R):
                @pl.when(jnp.logical_and(r < R - 1, r >= d))
                def _():
                    line_copy(kind, r - d, True).wait_send()

                @pl.when(jnp.logical_and(r > 0, r + d < R))
                def _():
                    line_copy(kind, r + d, False).wait_send()

    def p_copy(J):
        at = pl.ds(pl.multiple_of(J * BLOCK + (1 - c) * half, half), half)
        return remote(
            part.at[at, J * BLOCK:], part_in.at[J, :, J * BLOCK:], p_send.at[J], p_recv.at[J],
            (s, r, 1 - c),
        )

    def a_copy(o):
        return remote(
            cp.at[peer_s(o)], rs_a.at[o - 1], a_send.at[o - 1], a_recv.at[o - 1], (peer_s(o), r, c)
        )

    def held(J, q, core):
        return pl.ds(pl.multiple_of(J * BLOCK + core * half + q * n, n), n)

    def b_copy(J, q):
        return remote(
            dp.at[J, q * n:(q + 1) * n, J * BLOCK:], rs_b.at[J, s, :, J * BLOCK:],
            b_send.at[J, q], b_recv.at[J, s], (q, r, c),
        )

    def b_start(J):
        for q in range(owners):
            @pl.when(s != q)
            def _():
                b_copy(J, q).start()

    def g_copy(J, o, turn):
        return remote(
            rs_b.at[J, s, :, J * BLOCK:], aug.at[held(J, s, c), J * BLOCK:], g_send.at[J, o, turn], g_recv.at[J, s, c],
            (peer_s(o), r, lax.rem(c + turn, C)),
        )

    targets = [(o, turn) for o in range(S) for turn in range(C) if o or turn]

    def b_sum(J):
        @pl.when(s < owners)
        def _():
            at = pl.ds(pl.multiple_of(s * n, n), n)
            total = dp[J, at, J * BLOCK:]
            for o in range(1, S):
                p = peer_s(o)
                ref = rs_b.at[J, p, :, J * BLOCK:]
                remote(ref, ref, b_send.at[J, 0], b_recv.at[J, p], (s, r, 1 - c)).wait_recv()
                total += rs_b[J, p, :, J * BLOCK:]
            aug[held(J, s, c), J * BLOCK:] = total
            rs_b[J, s, :, J * BLOCK:] = total
            for o, turn in targets:
                g_copy(J, o, turn).start()

    def g_arrived(J):
        for q in range(owners):
            for core in range(C):
                @pl.when(jnp.logical_or(s != q, c != core))
                def _():
                    ref = aug.at[held(J, q, core), J * BLOCK:]
                    remote(
                        ref, ref, g_send.at[J, 0, 1], g_recv.at[J, q, core], (s, r, 1 - c)
                    ).wait_recv()

    def u_copy():
        return remote(upd.at[1 - c], upd_in, u_send, u_recv, (s, r, 1 - c))

    @pl.when(s == 0)
    def _():
        f_start()
    fetch(0).wait()
    fetch(1).wait()
    for j in range(slices):
        @pl.when(s == j)
        def _():
            columns[j] = factor[:, j * wide:(j + 1) * wide]

    @pl.when(s == 0)
    def _():
        roots[r] = root[...]
        for up in (True, False):
            line_start(parts, r, up)

    @pl.when(s < slices)
    def _():
        @pl.when(s != 0)
        def _():
            f_arrived(0)

        lead[mine_of(r), :] = columns[0]
        for kind in range(parts):
            for up in (True, False):
                line_start(kind, r, up)

    @pl.when(s != 0)
    def _():
        f_start()

    def solve(i):
        sol = mm(kinv[i], pb[i], 1, 0).astype(jnp.bfloat16)
        solved[i] = sol
        return sol

    fetch(2).wait()
    fetch(3).wait()
    for k in range(share):
        i = c * share + k
        term = mm(solve(i), pb[i], 0, 0)
        if k == 0:
            part[...] = term
        else:
            part[...] += term

    def hops(d):
        for kind in range(parts + 1):
            hop(kind, d)

    def others():
        for k in range(scenarios - share):
            solve(lax.rem((c + 1) * share + k, scenarios))

    def couple():
        fetch(4).wait()
        for g in range(groups):
            acc = mm(border[0, g], solved[0], 1, 0)
            for i in range(1, scenarios):
                acc += mm(border[i, g], solved[i], 1, 0)
            cp[g] = acc

    between = {1: others, 2: couple}
    for d in range(1, max(R, 3)):
        if d < R:
            hops(d)
        if d in between:
            between[d]()

    @pl.when(s == 0)
    def _():
        for q in range(R):
            at = pl.ds(pl.multiple_of((q * C + c) * own, own), own)
            part[at, :] += roots[q]

    @pl.when(s < slices)
    def _():
        part[...] -= mm(lead[...], lead[...], 1, 1)

    for J in range(blocks):
        p_copy(J).start()
    for J in range(blocks):
        p_copy(J).wait_recv()
        at = pl.ds(pl.multiple_of(J * BLOCK + c * half, half), half)
        dp[J, :, J * BLOCK:] = part[at, J * BLOCK:] + part_in[J, :, J * BLOCK:]
        b_start(J)
    b_sum(0)

    @pl.when(s < slices)
    def _():
        for q in range(S):
            @pl.when(s != q)
            def _():
                if q:
                    f_arrived(q)

            term = mm(columns[q], lead[...], 1, 1)
            for k in range(C):
                upd[k, q] = term[k * own:(k + 1) * own]
        u_copy().start()

    for J in range(1, blocks):
        b_sum(J)

    @pl.when(s < slices)
    def _():
        u_copy().wait()
        for q in range(S):
            cp[q] -= upd[c, q] + upd_in[q]

    for o in range(1, S):
        a_copy(o).start()
    down = lax.broadcasted_iota(jnp.int32, (BLOCK, BLOCK), 0)
    across = lax.broadcasted_iota(jnp.int32, (BLOCK, BLOCK), 1)
    eye = jnp.where(down == across, 1.0, 0.0).astype(F32)

    @pl.loop(0, blocks)
    def _(J):
        for j in range(blocks):
            @pl.when(J == j)
            def _():
                g_arrived(j)
                lo, hi = j * BLOCK, (j + 1) * BLOCK
                if j:
                    aug[lo:hi, lo:] -= mm_f32(aug[0:lo, lo:hi], aug[0:lo, lo:], 0, 0)

        at = pl.ds(pl.multiple_of(J * BLOCK, BLOCK), BLOCK)
        square = aug[at, at]
        work[:, 0:BLOCK] = jnp.where(down <= across, square, square.T)
        work[:, BLOCK:2 * BLOCK] = eye
        factor_block(work)
        inv[J] = work[:, BLOCK:2 * BLOCK]
        for j in range(blocks - 1):
            @pl.when(J == j)
            def _():
                lo, hi = j * BLOCK, (j + 1) * BLOCK
                aug[lo:hi, hi:] = mm_f32(inv[j], aug[lo:hi, hi:], 1, 0)

    acc = root[...] + cp[s]
    for o in range(1, S):
        a_copy(o).wait_recv()
        acc += rs_a[o - 1]
    rest[...] = acc
    for j in range(blocks):
        lo, hi = j * BLOCK, (j + 1) * BLOCK
        solution_block = mm_f32(rest[:, lo:hi], inv[j], 1, 1)
        out_ref[:, lo:hi] = solution_block
        if hi < panel:
            rest[:, hi:] -= mm_f32(solution_block, aug[lo:hi, hi:], 1, 0)

    for j in range(slices):
        @pl.when(s != j)
        def _():
            f_copy(j).wait_send()

    for kind in range(parts + 1):
        line_sent(kind)
    for J in range(blocks):
        p_copy(J).wait_send()
        for q in range(owners):
            @pl.when(s != q)
            def _():
                b_copy(J, q).wait_send()

        @pl.when(s < owners)
        def _():
            for o, turn in targets:
                g_copy(J, o, turn).wait_send()

    for o in range(1, S):
        a_copy(o).wait_send()


def panel_step(S, R, C, border, panel_border, kinv, factor, root):
    rows, depth = factor.shape
    own, panel = root.shape
    groups = border.shape[1]
    blocks = panel // BLOCK
    half = BLOCK // C
    n = max(half // S, 8)
    slices = min(S, SLICES)
    dma = pltpu.SemaphoreType.DMA
    bf16 = jnp.bfloat16
    vmem = pltpu.VMEM
    inputs = (border, panel_border, kinv, factor, root)
    return pl.pallas_call(
        functools.partial(panel_kernel, S, R, C, slices),
        out_shape=jax.ShapeDtypeStruct((own, panel), F32),
        in_specs=[pl.BlockSpec(memory_space=pl.ANY)] * len(inputs),
        out_specs=pl.BlockSpec(memory_space=pltpu.VMEM),
        scratch_shapes=[vmem(x.shape, x.dtype) for x in inputs] + [
            vmem((R * rows, depth // slices), bf16),
            vmem((R, own, panel), F32),
            vmem(kinv.shape, bf16),
            vmem((panel, panel), F32),
            vmem((blocks, half, panel), F32),
            vmem((groups, own, panel), F32),
            vmem((S - 1, own, panel), F32),
            vmem((blocks, half, panel), F32),
            vmem((blocks, S, n, panel), F32),
            vmem((S, rows, depth // slices), bf16),
            vmem((C, S, own, panel), F32),
            vmem((S, own, panel), F32),
            vmem((own, panel), F32),
            vmem((panel, panel), F32),
            vmem((BLOCK, 2 * BLOCK), F32),
            vmem((panel // BLOCK, BLOCK, BLOCK), F32),
            dma((len(inputs),)),
            dma((slices,)), dma((S,)),
            dma((3, R, 2)), dma((3, R)),
            dma((blocks,)), dma((blocks,)),
            dma((S - 1,)), dma((S - 1,)),
            dma((blocks, S)), dma((blocks, S)),
            dma((blocks, S, C)), dma((blocks, S, C)),
            dma, dma,
        ],
        compiler_params=pltpu.CompilerParams(
            collective_id=0, has_side_effects=True, vmem_limit_bytes=56 * 1024 * 1024
        ),
    )(*inputs)


def factor_block(work):
    size = work.shape[0]
    sub = lax.broadcasted_iota(jnp.int32, (STRIP, BLOCK), 0)
    for j in range(size // STRIP):
        lo = j * STRIP
        left = work[lo:lo + STRIP, 0:BLOCK]
        right = work[lo:lo + STRIP, BLOCK:2 * BLOCK]
        cols = [
            jnp.broadcast_to(left[:, lo + b:lo + b + 1], (STRIP, BLOCK)) for b in range(STRIP)
        ]
        scale = jnp.zeros((STRIP, BLOCK), F32)
        for k in range(0, STRIP, 2):
            one, two = cols[k], cols[k + 1]
            a = jnp.broadcast_to(one[k:k + 1, :], (STRIP, BLOCK))
            b = jnp.broadcast_to(two[k:k + 1, :], (STRIP, BLOCK))
            d = jnp.broadcast_to(two[k + 1:k + 2, :], (STRIP, BLOCK))
            det = a * d - b * b
            inverse = pl.reciprocal(det, approx=True)
            refine = 2.0 - det * inverse
            first = pl.reciprocal(a, approx=True)
            first = first * (2.0 - a * first)
            scale = jnp.where(sub == k, lax.rsqrt(a), scale)
            scale = jnp.where(sub == k + 1, lax.rsqrt(det * first), scale)
            times = jnp.where(sub == k + 1, b * first, 0.0)
            if k + 2 < STRIP:
                times_one = (jnp.where(sub > k + 1, one * d - two * b, 0.0) * inverse) * refine
                times_two = (jnp.where(sub > k + 1, two * a - one * b, 0.0) * inverse) * refine
                for q in range(k + 2, STRIP):
                    cols[q] = cols[q] - (
                        times_one * cols[q][k:k + 1, :] + times_two * cols[q][k + 1:k + 2, :]
                    )
                times = times + times_one
                left, right = (
                    x - (times * x[k:k + 1, :] + times_two * x[k + 1:k + 2, :]) for x in (left, right)
                )
            else:
                left, right = (x - times * x[k:k + 1, :] for x in (left, right))
        left = left * scale
        right = right * scale
        work[lo:lo + STRIP, 0:BLOCK] = left
        work[lo:lo + STRIP, BLOCK:2 * BLOCK] = right
        if lo + STRIP < size:
            both = jnp.concatenate([left, right], axis=1)
            work[lo + STRIP:, :] -= mm_f32(left, both, 0, 0)[lo + STRIP:, :]


def solution(mesh):
    S, R, C = mesh.shape["scen"], mesh.shape["row"], mesh.shape["col"]
    in_specs = (
        P("scen", None, ("row", "col"), None),
        P("scen", None, None),
        P("scen", None, None),
        P(("scen", "row"), "col"),
        P(("scen", "row", "col"), None),
    )
    out_specs = P(("scen", "row", "col"), None)

    def per_device(border, panel_border, kinv, factor, root_block):
        return panel_step(S, R, C, border, panel_border, kinv, factor, root_block)

    return jax.shard_map(
        per_device, mesh=mesh, in_specs=in_specs, out_specs=out_specs, check_vma=False
    )
```

profile of v0, /device:TPU:0, one launch (start us, length us, event | category | flops | bytes accessed | tf_op | source)
XLA Modules:
  0.0 56.1 jit_solution(5185949711493789277)
XLA Ops:
  0.0 54.5 %shard_map.55 = f32[64,512]{1,0:T(8,128)} custom-call(bf16[4,4,64,512]{3,2,1,0:T(8,128)(2,1)} %border_hbm.1, bf16[4,512,512]{2,1,0:T(8,128)(2,1)} %pb_hbm.1, bf16[4,512,512]{2,1,0:T(8,128)(2,1)} %kinv_hbm.1, bf16[128,2048]{1,0:T(8,128)(2,1)} %factor_hbm.1, f32[64,512]{1,0:T(8,128)} %root_hbm.1), custom_call_target="tpu_custom_call" | custom-call | tf_op jit(solution)/shard_map/pallas_call | solution.py:393
  54.5 1.6 %copy.7 = f32[64,512]{1,0:T(8,128)} copy(f32[64,512]{1,0:T(8,128)} %shard_map.55) | data formatting | bytes 262144
where the time goes:
time: 56.2 us; the launch traced here: 56.1 us
  Pallas kernels  54.5 us (97%)
  local copies, waits for them, and re-layouts  1.57 us (3%)
    pallas_call x1, Pallas kernels, panel_step(): pl.pallas_call(functools.partial(panel_kernel, S, R, C, slices), out_shap...  54.5 us
    unnamed x1, local copies, waits for them, and re-layouts  1.57 us

commit v1 on v0

--- a/solution.py
+++ b/solution.py
@@ -293,33 +293,35 @@
         b_start(J)
     b_sum(0)
 
-    @pl.when(s < slices)
-    def _():
-        for q in range(S):
-            @pl.when(s != q)
-            def _():
-                if q:
-                    f_arrived(q)
-
-            term = mm(columns[q], lead[...], 1, 1)
-            for k in range(C):
-                upd[k, q] = term[k * own:(k + 1) * own]
-        u_copy().start()
-
     for J in range(1, blocks):
         b_sum(J)
 
-    @pl.when(s < slices)
-    def _():
-        u_copy().wait()
-        for q in range(S):
-            cp[q] -= upd[c, q] + upd_in[q]
-
-    for o in range(1, S):
-        a_copy(o).start()
+    def update():
+        @pl.when(s < slices)
+        def _():
+            for q in range(S):
+                @pl.when(s != q)
+                def _():
+                    if q:
+                        f_arrived(q)
+
+                term = mm(columns[q], lead[...], 1, 1)
+                for k in range(C):
+                    upd[k, q] = term[k * own:(k + 1) * own]
+            u_copy().start()
+
+    def send_terms():
+        @pl.when(s < slices)
+        def _():
+            u_copy().wait()
+            for q in range(S):
+                cp[q] -= upd[c, q] + upd_in[q]
+
+        for o in range(1, S):
+            a_copy(o).start()
+
     down = lax.broadcasted_iota(jnp.int32, (BLOCK, BLOCK), 0)
     across = lax.broadcasted_iota(jnp.int32, (BLOCK, BLOCK), 1)
-    eye = jnp.where(down == across, 1.0, 0.0).astype(F32)
 
     @pl.loop(0, blocks)
     def _(J):
@@ -328,15 +330,18 @@
             def _():
                 g_arrived(j)
                 lo, hi = j * BLOCK, (j + 1) * BLOCK
+                if j == min(1, blocks - 1):
+                    update()
+                if j == min(2, blocks - 1):
+                    send_terms()
                 if j:
                     aug[lo:hi, lo:] -= mm_f32(aug[0:lo, lo:hi], aug[0:lo, lo:], 0, 0)
 
         at = pl.ds(pl.multiple_of(J * BLOCK, BLOCK), BLOCK)
         square = aug[at, at]
-        work[:, 0:BLOCK] = jnp.where(down <= across, square, square.T)
-        work[:, BLOCK:2 * BLOCK] = eye
+        work[...] = jnp.where(down <= across, square, square.T)
         factor_block(work)
-        inv[J] = work[:, BLOCK:2 * BLOCK]
+        inv[J] = jnp.where(down >= across, work[...], 0.0)
         for j in range(blocks - 1):
             @pl.when(J == j)
             def _():
@@ -410,7 +415,7 @@
             vmem((S, own, panel), F32),
             vmem((own, panel), F32),
             vmem((panel, panel), F32),
-            vmem((BLOCK, 2 * BLOCK), F32),
+            vmem((BLOCK, BLOCK), F32),
             vmem((panel // BLOCK, BLOCK, BLOCK), F32),
             dma((len(inputs),)),
             dma((slices,)), dma((S,)),
@@ -430,13 +435,16 @@
 def factor_block(work):
     size = work.shape[0]
     sub = lax.broadcasted_iota(jnp.int32, (STRIP, BLOCK), 0)
+    lane = lax.broadcasted_iota(jnp.int32, (STRIP, BLOCK), 1)
+    across = lax.broadcasted_iota(jnp.int32, (BLOCK, BLOCK), 1)
     for j in range(size // STRIP):
         lo = j * STRIP
-        left = work[lo:lo + STRIP, 0:BLOCK]
-        right = work[lo:lo + STRIP, BLOCK:2 * BLOCK]
+        left = work[lo:lo + STRIP, :]
         cols = [
             jnp.broadcast_to(left[:, lo + b:lo + b + 1], (STRIP, BLOCK)) for b in range(STRIP)
         ]
+        inside = jnp.logical_and(lane >= lo, lane < lo + STRIP)
+        strip = jnp.where(lane - lo == sub, 1.0, jnp.where(inside, 0.0, left))
         scale = jnp.zeros((STRIP, BLOCK), F32)
         for k in range(0, STRIP, 2):
             one, two = cols[k], cols[k + 1]
@@ -459,18 +467,15 @@
                         times_one * cols[q][k:k + 1, :] + times_two * cols[q][k + 1:k + 2, :]
                     )
                 times = times + times_one
-                left, right = (
-                    x - (times * x[k:k + 1, :] + times_two * x[k + 1:k + 2, :]) for x in (left, right)
-                )
+                strip = strip - (times * strip[k:k + 1, :] + times_two * strip[k + 1:k + 2, :])
             else:
-                left, right = (x - times * x[k:k + 1, :] for x in (left, right))
-        left = left * scale
-        right = right * scale
-        work[lo:lo + STRIP, 0:BLOCK] = left
-        work[lo:lo + STRIP, BLOCK:2 * BLOCK] = right
+                strip = strip - times * strip[k:k + 1, :]
+        strip = strip * scale
+        work[lo:lo + STRIP, :] = strip
         if lo + STRIP < size:
-            both = jnp.concatenate([left, right], axis=1)
-            work[lo + STRIP:, :] -= mm_f32(left, both, 0, 0)[lo + STRIP:, :]
+            below = work[lo + STRIP:, :]
+            gone = jnp.logical_and(across[lo + STRIP:] >= lo, across[lo + STRIP:] < lo + STRIP)
+            work[lo + STRIP:, :] = jnp.where(gone, 0.0, below) - mm_f32(strip, strip, 0, 0)[lo + STRIP:, :]
 
 
 def solution(mesh):

time: 56.2 us -> 57.2 us (1.018)
  Pallas kernels: 54.5 us -> 55.5 us
    pallas_call x1, Pallas kernels: 54.5 us -> 55.5 us  [panel_step(): pl.pallas_call(functools.partial(panel_kernel, S, R, C, slices), out_shap...]
where the time goes in v1:
time: 57.2 us; the launch traced here: 57.1 us
  Pallas kernels  55.5 us (97%)
  local copies, waits for them, and re-layouts  1.57 us (3%)
    pallas_call x1, Pallas kernels, panel_step(): pl.pallas_call(functools.partial(panel_kernel, S, R, C, slices), out_shap...  55.5 us
    unnamed x1, local copies, waits for them, and re-layouts  1.57 us

profile of v1, /device:TPU:0, one launch (start us, length us, event | category | flops | bytes accessed | tf_op | source)
XLA Modules:
  0.0 57.1 jit_solution(15430400508582644048)
XLA Ops:
  0.0 55.5 %shard_map.55 = f32[64,512]{1,0:T(8,128)} custom-call(bf16[4,4,64,512]{3,2,1,0:T(8,128)(2,1)} %border_hbm.1, bf16[4,512,512]{2,1,0:T(8,128)(2,1)} %pb_hbm.1, bf16[4,512,512]{2,1,0:T(8,128)(2,1)} %kinv_hbm.1, bf16[128,2048]{1,0:T(8,128)(2,1)} %factor_hbm.1, f32[64,512]{1,0:T(8,128)} %root_hbm.1), custom_call_target="tpu_custom_call" | custom-call | tf_op jit(solution)/shard_map/pallas_call | solution.py:398
  55.5 1.6 %copy.7 = f32[64,512]{1,0:T(8,128)} copy(f32[64,512]{1,0:T(8,128)} %shard_map.55) | data formatting | bytes 262144
